TPU v7x, 128 devices: a whole 4x4x4 slice. The times are simulated.
128 devices in a mesh: row: 8 (over y_lo, x), col: 16 (over z, y_hi, core).
Axes of the slice: x: 4, y: 4 (y_hi: 2, y_lo: 2; y = y_hi * 2 + y_lo), z: 4, core: 2. Of those that a mesh axis runs over, the one named last changes fastest.
Arguments:
- front_init: float32 [4, 8, 2, 16, 512, 512], P(None, 'row', None, 'col'), as said below
- child_tiles: bfloat16 [8, 16, 8, 512, 512], P('row', 'col'), may hold values from -0.29882812 to 0.29882812
- child_map: int32 [8, 16, 8, 2], replicated, may hold values from 0 to 31, as said below
- child_counts: int32 [8, 16], replicated, may hold values from 5 to 8
- child_extent: int32 [8, 16, 8], replicated, may hold values from 128 to 512
Outputs:
- schur: float32 [4, 8, 2, 16, 512, 512], P(None, 'row', None, 'col')
- panel: float32 [4, 8, 512, 512], P(None, 'row')
Inputs may be any that keep to these rules, and one draw needn't show every extreme that they name: child_map[r, c, s, 0] is congruent to r modulo 8; the live slots of one grid position name tile columns that are all different modulo 16; in every process row some process column receives a live slot from every position of that row. `front_init`: the symmetric part of tile (0, 0) of assembled is positive definite.
All inputs are finite; a program needn't handle non-finite values.
Results may differ from a plain program's by a relative error of at most 0.00045.
Values may be sent and summed in bfloat16 or wider, within the bound.
A program may use at most 128 MiB of HBM per device.

v0:
```python
import jax
import jax.numpy as jnp
from jax import lax
from jax.sharding import PartitionSpec as P


def from_root(value, axis, root):
    mine = lax.axis_index(axis) == root
    return lax.psum(jnp.where(mine, value, jnp.zeros_like(value)), axis)


def per_device(front_init, child_tiles, child_map, child_counts, child_extent):
    grid_rows = lax.axis_size("row")
    grid_cols = lax.axis_size("col")
    row_index = lax.axis_index("row")
    col_index = lax.axis_index("col")
    rows_here = front_init.shape[0]
    cols_here = front_init.shape[2]
    edge_len = front_init.shape[-1]
    slot_count = child_tiles.shape[2]
    local_front = front_init.reshape(rows_here, cols_here, edge_len, edge_len)
    own_tiles = child_tiles.reshape(slot_count, edge_len, edge_len)
    row_maps = lax.dynamic_index_in_dim(child_map, row_index, 0, False)
    row_counts = lax.dynamic_index_in_dim(child_counts, row_index, 0, False)
    own_map = lax.dynamic_index_in_dim(row_maps, col_index, 0, False)
    own_count = lax.dynamic_index_in_dim(row_counts, col_index, 0, False)
    own_extent = lax.dynamic_index_in_dim(
        lax.dynamic_index_in_dim(child_extent, row_index, 0, False), col_index, 0, False
    )
    slot_ids = jnp.arange(slot_count, dtype=jnp.int32)
    peer_ids = jnp.arange(grid_cols, dtype=jnp.int32)
    chosen = (own_map[None, :, 1] % grid_cols == peer_ids[:, None]) & (
        slot_ids[None, :] < own_count
    )
    has_tile = jnp.any(chosen, axis=1)
    which_slot = jnp.sum(jnp.where(chosen, slot_ids[None, :], 0), axis=1)
    picked = jnp.take(own_tiles, which_slot, axis=0)
    limits_out = jnp.take(own_extent, which_slot)
    offsets = jnp.arange(edge_len, dtype=jnp.int32)
    inside = (
        (offsets[None, :, None] < limits_out[:, None, None])
        & (offsets[None, None, :] < limits_out[:, None, None])
        & has_tile[:, None, None]
    )
    outgoing = jnp.where(inside, picked, jnp.zeros((), picked.dtype))
    source_cols = row_maps[:, :, 1]
    source_alive = (source_cols % grid_cols == col_index) & (
        slot_ids[None, :] < row_counts[:, None]
    )
    local_slot = row_maps[:, :, 0] // grid_rows * cols_here + source_cols // grid_cols
    places = jnp.arange(rows_here * cols_here, dtype=jnp.int32)
    placing = jnp.sum(
        ((local_slot[None] == places[:, None, None]) & source_alive[None]).astype(jnp.float32),
        axis=2,
    ).astype(jnp.bfloat16)
    added = jnp.einsum(
        "lq,qky->lky",
        placing,
        lax.all_to_all(outgoing, "col", split_axis=0, concat_axis=0, tiled=True),
        preferred_element_type=jnp.float32,
    )
    assembled = local_front + added.reshape(rows_here, cols_here, edge_len, edge_len)
    column_block = assembled[:, 0]
    diagonal = from_root(column_block[0], "row", 0)
    factor = jnp.linalg.cholesky(diagonal)
    solved = jax.scipy.linalg.solve_triangular(
        factor, column_block.reshape(rows_here * edge_len, edge_len).T, lower=True
    ).T
    solved = solved.reshape(rows_here, edge_len, edge_len)
    is_first = (jnp.arange(rows_here, dtype=jnp.int32) == 0) & (row_index == 0)
    own_panel = jnp.where(is_first[:, None, None], factor[None], solved)
    panel_rows = from_root(own_panel, "col", 0)
    stride = grid_cols // grid_rows
    root_row = col_index % grid_rows
    needed = jnp.arange(cols_here, dtype=jnp.int32) * stride + col_index // grid_rows
    col_panel = jnp.take(
        from_root(panel_rows.astype(jnp.bfloat16), "row", root_row).astype(panel_rows.dtype),
        needed,
        axis=0,
    )
    update = jnp.einsum(
        "axk,byk->abxy",
        panel_rows,
        col_panel,
        precision=lax.Precision.HIGHEST,
        preferred_element_type=jnp.float32,
    )
    tile_rows = jnp.arange(rows_here, dtype=jnp.int32) * grid_rows + row_index
    tile_cols = jnp.arange(cols_here, dtype=jnp.int32) * grid_cols + col_index
    keep_tile = (tile_rows[:, None] > 0) & (tile_cols[None, :] > 0)
    schur_part = jnp.where(keep_tile[:, :, None, None], assembled - update, jnp.float32(0.0))
    return (
        schur_part.reshape(rows_here, 1, cols_here, 1, edge_len, edge_len),
        panel_rows.reshape(rows_here, 1, edge_len, edge_len),
    )


def solution(mesh):
    in_specs = (
        P(None, "row", None, "col", None, None),
        P("row", "col", None, None, None),
        P(),
        P(),
        P(),
    )
    out_specs = (P(None, "row", None, "col", None, None), P(None, "row", None, None))
    return jax.shard_map(
        per_device, mesh=mesh, in_specs=in_specs, out_specs=out_specs, check_vma=False
    )
```

profile of v0, /device:TPU:72, one launch (start us, length us, event | category | flops | bytes accessed | tf_op | source)
XLA Modules:
  0.0 686.3 jit_solution(2868427694036610174)
XLA Ops:
  11.2 7.1 %gather_fusion.1 = bf16[16,512,512]{2,1,0:T(8,128)(2,1)} fusion(bf16[8,512,512]{2,1,0:T(8,128)(2,1)} %bitcast.125, s32[1024]{0:T(1024)S(1)} %pad_clamp_fusion.1), kind=kCustom, calls=%fused_computation.1 | custom fusion | bytes 16777280 | tf_op jit(solution)/shard_map/jit(_take)/gather | solution.py:37
  18.2 8.9 %and_select_fusion = bf16[16,512,512]{2,1,0:T(8,128)(2,1)} fusion(bf16[16,512,512]{2,1,0:T(8,128)(2,1)} %gather_fusion.1, pred[16]{0:T(512)(128)(4,1)S(1)} %get-tuple-element.31, pred[16]{0:T(512)(128)(4,1)S(1)} %fusion.55, pred[16,512]{1,0:T(8,128)(4,1)S(1)} %iota_compare_fusion.3), kind=kLoop, calls=%fused_computation.5 | loop fusion | flops 16777216 | bytes 16785440 | tf_op jit(solution)/shard_map/jit(_where)/select_n | solution.py:45
  27.2 6.6 all-to-all-start
  33.9 9.9 %copy.46 = f32[4,1,2,1,512,512]{4,5,2,0,3,1:T(8,128)} copy(f32[4,1,2,1,512,512]{5,4,3,2,1,0:T(8,128)} %param.5) | data formatting | bytes 16777216 | tf_op args[0]
  44.5 83.6 %all-to-all-done = bf16[16,512,512]{2,1,0:T(8,128)(2,1)} async-done(((bf16[16,512,512]{2,1,0:T(8,128)(2,1)}), bf16[16,512,512]{2,1,0:T(8,128)(2,1)}, u32[]{:S(2)}, u32[]{:S(2)}) %all-to-all-start) | async-done | bytes 8388640 | tf_op jit(solution)/shard_map/all_to_all | solution.py:59
  128.1 11.5 %fusion.2 = f32[8,512,512]{2,0,1:T(8,128)} fusion(bf16[16,512,512]{2,1,0:T(8,128)(2,1)} %all-to-all-done, bf16[8,16]{1,0:T(8,128)(2,1)S(1)} %convert_reduce_fusion), kind=kOutput, calls=%fused_computation.10 | convolution fusion | flops 67108864 | bytes 16777472 | tf_op jit(solution)/shard_map/lq,qky->lky/dot_general | solution.py:56
  139.6 9.9 %copy.50 = f32[8,512,512]{1,2,0:T(8,128)} copy(f32[8,512,512]{2,0,1:T(8,128)} %fusion.2) | data formatting | bytes 16777216 | tf_op jit(solution)/shard_map/lq,qky->lky/dot_general | solution.py:56
  149.5 11.3 %bitcast_add_fusion = f32[4,2,512,512]{2,3,1,0:T(8,128)} fusion(f32[4,2,512,512]{2,3,1,0:T(8,128)} %bitcast.124, f32[4,1,2,1,512,512]{4,5,2,0,3,1:T(8,128)} %copy.46), kind=kLoop, calls=%fused_computation.9 | loop fusion | flops 2097152 | bytes 25165824 | tf_op jit(solution)/shard_map/add | solution.py:62
  163.2 4.6 slice.156
  167.9 5.2 copy.52
  173.1 5.8 copy.53
  178.9 61.1 %all-reduce.5.cloned.1.call-done = f32[512,512]{0,1:T(8,128)} async-done(((f32[512,512]{0,1:T(8,128)}), f32[512,512]{0,1:T(8,128)}) %all-reduce.5.cloned.1.call-update) | async-done | bytes 1048592 | tf_op jit(solution)/shard_map/psum | solution.py:9
  243.0 11.7 %cholesky.103 = f32[128,128]{1,0:T(8,128)S(1)} custom-call(f32[128,128]{1,0:T(8,128)S(1)} %cholesky.263), custom_call_target="Cholesky" | custom-call | tf_op jit(solution)/shard_map/jit(cholesky)/cholesky | solution.py:65
  254.8 9.8 %custom-call.31 = f32[1,128,128]{1,2,0:T(8,128)S(1)} custom-call(f32[1,128,128]{2,1,0:T(8,128)S(1)} %get-tuple-element.43), custom_call_target="InvertDiagBlocksLowerTriangular" | custom-call | tf_op jit(solution)/shard_map/jit(cholesky)/cholesky | solution.py:65
  265.4 11.7 %cholesky.215 = f32[128,128]{1,0:T(8,128)S(1)} custom-call(f32[128,128]{1,0:T(8,128)S(1)} %cholesky.267), custom_call_target="Cholesky" | custom-call | tf_op jit(solution)/shard_map/jit(cholesky)/cholesky | solution.py:65
  277.1 10.0 %custom-call.32 = f32[1,128,128]{1,2,0:T(8,128)S(1)} custom-call(f32[1,128,128]{2,1,0:T(8,128)S(1)} %get-tuple-element.40), custom_call_target="InvertDiagBlocksLowerTriangular" | custom-call | tf_op jit(solution)/shard_map/jit(cholesky)/cholesky | solution.py:65
  287.8 11.7 %cholesky.236 = f32[128,128]{1,0:T(8,128)S(1)} custom-call(f32[128,128]{1,0:T(8,128)S(1)} %cholesky.272), custom_call_target="Cholesky" | custom-call | tf_op jit(solution)/shard_map/jit(cholesky)/cholesky | solution.py:65
  300.2 9.8 %custom-call.33 = f32[1,128,128]{1,2,0:T(8,128)S(1)} custom-call(f32[1,128,128]{2,1,0:T(8,128)S(1)} %get-tuple-element.37), custom_call_target="InvertDiagBlocksLowerTriangular" | custom-call | tf_op jit(solution)/shard_map/jit(cholesky)/cholesky | solution.py:65
  310.6 11.7 %cholesky.253 = f32[128,128]{1,0:T(8,128)S(1)} custom-call(f32[128,128]{1,0:T(8,128)S(1)} %convolution_subtract_fusion.4), custom_call_target="Cholesky" | custom-call | tf_op jit(solution)/shard_map/jit(cholesky)/cholesky | solution.py:65
  326.7 8.1 %while.1 = (s32[]{:T(128)}, f32[512,512]{1,0:T(8,128)S(1)}, s32[4,2]{0,1:T(2,128)S(1)}, f32[4,128,128]{2,1,0:T(8,128)S(1)}, s32[]{:T(128)}) while((s32[]{:T(128)}, f32[512,512]{1,0:T(8,128)S(1)}, s32[4,2]{0,1:T(2,128)S(1)}, f32[4,128,128]{2,1,0:T(8,128)S(1)}, s32[]{:T(128)}) %tuple.39), condition=%wide.while_cond, body=%wide.while_body.sunk | while | flops 2 | bytes 131189 | solution.py:66
  334.9 39.3 %custom-call.34 = f32[4,128,128]{1,2,0:T(8,128)S(1)} custom-call(f32[4,128,128]{2,1,0:T(8,128)S(1)} %get-tuple-element.9), custom_call_target="InvertDiagBlocksLowerTriangular" | custom-call | tf_op jit(solution)/shard_map/jit(_solve_triangular)/triangular_solve | solution.py:66
  385.4 2.5 maximum_bitcast_fusion
  387.9 5.3 copy.58
  393.2 4.9 select_select_fusion
  398.5 147.7 %all-reduce.7.cloned.1.call-done = f32[4,512,512]{2,1,0:T(8,128)} async-done(((f32[4,512,512]{2,1,0:T(8,128)}), f32[4,512,512]{2,1,0:T(8,128)}) %all-reduce.7.cloned.1.call-update) | async-done | bytes 4194320 | tf_op jit(solution)/shard_map/psum | solution.py:9
  546.2 3.7 convert_select_fusion
  550.1 90.4 %all-reduce.9.cloned.1.call-done = bf16[4,512,512]{2,1,0:T(8,128)(2,1)} async-done(((bf16[4,512,512]{2,1,0:T(8,128)(2,1)}), bf16[4,512,512]{2,1,0:T(8,128)(2,1)}) %all-reduce.9.cloned.1.call-update) | async-done | bytes 2097168 | tf_op jit(solution)/shard_map/psum | solution.py:9
  640.4 4.2 convert_element_type.15
  644.6 2.9 gather_fusion.2
  647.5 17.3 %fusion.1 = f32[4,1,2,1,512,512]{4,5,2,0,3,1:T(8,128)} fusion(f32[4,2,512,512]{2,3,1,0:T(8,128)} %bitcast_add_fusion, pred[4,2]{1,0:T(4,128)(4,1)S(1)} %broadcast_and_fusion, f32[4,512,512]{2,1,0:T(8,128)} %all-reduce.7.cloned.1.call-done, f32[2,512,512]{2,1,0:T(8,128)S(1)} %gather_fusion.2, pred[2]{0:T(512)(128)(4,1)S(1)} %get-tuple-element.46), kind=kOutput, calls=%fused_computation.8 | convolution fusion | flops 12889620480 | bytes 23068682 | tf_op jit(solution)/shard_map/axk,byk->abxy/dot_general | solution.py:81
  664.8 9.9 %copy.55 = f32[4,1,2,1,512,512]{5,4,3,2,1,0:T(8,128)} copy(f32[4,1,2,1,512,512]{4,5,2,0,3,1:T(8,128)} %fusion.1) | data formatting | bytes 16777216
  674.7 4.7 copy.79
  (80 shorter events, 34.4 us)
Async XLA Ops:
  7.2 2.0 copy-start
  27.2 100.9 %all-to-all-start = ((bf16[16,512,512]{2,1,0:T(8,128)(2,1)}), bf16[16,512,512]{2,1,0:T(8,128)(2,1)}, u32[]{:S(2)}, u32[]{:S(2)}) async-start(bf16[16,512,512]{2,1,0:T(8,128)(2,1)} %and_select_fusion), calls=%async_computation | async-start | bytes 16777216 | tf_op jit(solution)/shard_map/all_to_all | solution.py:59
  33.8 206.2 %all-reduce.5.cloned.1.call-start = ((), (), s32[]{:S(2)}) async-start(), calls=%async_computation.1 | async-start | bytes 2097152 | tf_op jit(solution)/shard_map/psum | solution.py:9
  163.1 383.1 %all-reduce.7.cloned.1.call-start = ((), (), s32[]{:S(2)}) async-start(), calls=%async_computation.2 | async-start | bytes 8388608 | tf_op jit(solution)/shard_map/psum | solution.py:9
  374.2 5.7 copy-start.2
  398.2 242.3 %all-reduce.9.cloned.1.call-start = ((), (), s32[]{:S(2)}) async-start(), calls=%async_computation.3 | async-start | bytes 4194304 | tf_op jit(solution)/shard_map/psum | solution.py:9
  674.7 4.7 copy-start.1
Sparse Core Ops, SparseCore 0:
  163.2 76.6 all-reduce.4
  398.3 147.8 all-reduce.6
  550.0 90.3 all-reduce.8
where the time goes:
time: 698 us; the launch traced here: 686 us
  waiting for transfers between devices  383 us (55%)
  other arithmetic  159 us (23%)
  local copies, waits for them, and re-layouts  78.8 us (11%)
  matrix products  41.8 us (6%)
  between operations  17.1 us (2%)
  starting transfers between devices  6.98 us (1%)
    psum x3, waiting for transfers between devices, from_root(): return lax.psum(jnp.where(mine, value, jnp.zeros_like(value)), axis)  299 us
    all_to_all x1, waiting for transfers between devices, per_device(): lax.all_to_all(outgoing, 'col', split_axis=0, concat_axis=0, tiled=True)  83.6 us
    another operation x14, other arithmetic, per_device(): factor = jnp.linalg.cholesky(diagonal)  78.6 us
    another operation x3, other arithmetic, per_device(): jax.scipy.linalg.solve_triangular(factor, column_block.reshape(rows_here...  39.8 us
    unnamed x9, local copies, waits for them, and re-layouts  24.5 us
    dot_general x1, matrix products, per_device(): jnp.einsum('axk,byk->abxy', panel_rows, col_panel, precision=lax.Precisio...  17.3 us
  transfers between devices with their start and end apart: 4, of which 4 were waited for; matrix products, arithmetic and copies ran while one was open for 4% of the time, Pallas kernels for 0%

commit v1 on v0

v1 whole, which is shorter than its diff:
```python
import functools

import jax
import jax.numpy as jnp
from jax import lax
from jax.experimental import pallas as pl
from jax.experimental.pallas import tpu as pltpu
from jax.sharding import PartitionSpec as P

MESH = pl.DeviceIdType.MESH
HIGH = lax.Precision.HIGHEST
F32 = jnp.float32
BF16 = jnp.bfloat16
B = 512
NB = 128
SLICE = 32
COLS = 16
ROWS = 8


def dot_nt(a, b, precision=HIGH):
    return lax.dot_general(
        a, b, (((1,), (1,)), ((), ())), precision=precision, preferred_element_type=F32
    )


def dot_nn(a, b, precision=HIGH):
    return lax.dot_general(
        a, b, (((1,), (0,)), ((), ())), precision=precision, preferred_element_type=F32
    )


def wide(x):
    return jnp.broadcast_to(x, (8, NB))


def factor_block(s):
    lane = lax.broadcasted_iota(jnp.int32, (8, NB), 1)
    sub = lax.broadcasted_iota(jnp.int32, (8, NB), 0)
    groups = NB // 8
    rows = [s[8 * p : 8 * p + 8, :] for p in range(groups)]
    eye = [jnp.where(lane == sub + 8 * p, 1.0, 0.0).astype(F32) for p in range(groups)]
    out_u, out_v = [], []
    for p in range(groups):
        r, e = rows[p], eye[p]
        cols = [wide(r[:, 8 * p + t : 8 * p + t + 1]) for t in range(8)]
        inv = [jnp.where(sub == t, 1.0, 0.0).astype(F32) for t in range(8)]
        pivots = None
        for t in range(8):
            pivot = wide(cols[t][t : t + 1, :])
            pivots = pivot if t == 0 else jnp.where(sub == t, pivot, pivots)
            m = jnp.where(sub > t, cols[t], 0.0) * (1.0 / pivot)
            for j in range(t + 1, 8):
                cols[j] = cols[j] - m * wide(cols[j][t : t + 1, :])
            for j in range(t + 1):
                inv[j] = inv[j] - m * wide(inv[j][t : t + 1, :])
        scale = lax.rsqrt(pivots)
        u = jnp.zeros_like(r)
        v = jnp.zeros_like(e)
        for t in range(8):
            u = u + inv[t] * wide(r[t : t + 1, :])
            v = v + inv[t] * wide(e[t : t + 1, :])
        u = u * scale
        v = v * scale
        out_u.append(jnp.where(lane >= sub + 8 * p, u, 0.0))
        out_v.append(v)
        if p < groups - 1:
            ut = jnp.transpose(u)
            for q in range(p + 1, groups):
                coef = ut[8 * q : 8 * q + 8, :]
                for t in range(8):
                    c = wide(coef[:, t : t + 1])
                    rows[q] = rows[q] - c * wide(u[t : t + 1, :])
                    eye[q] = eye[q] - c * wide(v[t : t + 1, :])
    return jnp.concatenate(out_u, 0), jnp.concatenate(out_v, 0)


def factor_step(j, s, l_ref, v_ref):
    a, b = NB * j, NB * j + NB
    u, v = factor_block(s[a:b, a:b])
    l_ref[a:b, a:b] = jnp.transpose(u)
    v_ref[a:b, a:b] = v
    if j:
        w = dot_nn(l_ref[a:b, 0:a], v_ref[0:a, 0:a])
        v_ref[a:b, 0:a] = -dot_nn(v, w)
    if b < B:
        low = dot_nt(s[b:B, a:b], v)
        l_ref[b:B, a:b] = low
        s[b:B, b:B] = s[b:B, b:B] - dot_nt(low, low)


def main_kernel(
    tab,
    kids_hbm,
    front_hbm,
    land,
    panel_hbm,
    need_hbm,
    kids,
    bucket,
    land0,
    fslice,
    pivot,
    col0,
    s,
    l_ref,
    v_ref,
    panel,
    own_need,
    loc,
    cut_s,
    cut_r,
    fs_s,
    fs_r,
    pr_s,
    pr_r,
    pg_s,
    pg_r,
    px,
    ag_s,
    ag_r,
    ax,
    bk_s,
    bk_r,
    nd_s,
    nd_r,
):
    row = lax.axis_index("row")
    col = lax.axis_index("col")
    zy = col // 2
    core = col % 2

    def remote(src, dst, ss, rs, to):
        return pltpu.make_async_remote_copy(
            src_ref=src, dst_ref=dst, send_sem=ss, recv_sem=rs, device_id=to, device_id_type=MESH
        )

    def mate(d):
        return lax.rem(col + d, COLS)

    def kin(d):
        return lax.rem(zy + d, ROWS)

    def fellow(d):
        return lax.rem(row + d, ROWS)

    sibling = (row, zy * 2 + 1 - core)

    load = pltpu.make_async_copy(kids_hbm, kids, loc.at[0])
    load.start()

    barrier = pltpu.get_barrier_semaphore()

    @pl.loop(1, COLS)
    def _(d):
        pl.semaphore_signal(barrier, inc=1, device_id=(row, mate(d)), device_id_type=MESH)

    @pl.loop(1, ROWS)
    def _(d):
        pl.semaphore_signal(barrier, inc=1, device_id=(fellow(d), col), device_id_type=MESH)

    pl.semaphore_wait(barrier, COLS - 1 + ROWS - 1)

    def front_part(k):
        return front_hbm.at[:, 0, pl.ds(pl.multiple_of(k * SLICE, SLICE), SLICE), :]

    def front_cut(d):
        return remote(front_part(mate(d)), fslice, fs_s.at[d], fs_r, (row, mate(d)))

    front_own = pltpu.make_async_copy(front_part(col), fslice, loc.at[1])

    @pl.when(col == 0)
    def _():
        front_own.start()

        @pl.loop(1, COLS)
        def _(d):
            front_cut(d).start()

    load.wait()

    def pack(k):
        slot = (tab[col, k] >> 16) & 7

        @pl.loop(0, 4)
        def _(q):
            part = pl.ds(pl.multiple_of(q * NB, NB), NB)
            bucket[k, part, :] = kids[slot, part, :]

    pack(0)

    def cut(d):
        k = mate(d)
        return remote(
            bucket.at[0, pl.ds(pl.multiple_of(k * SLICE, SLICE), SLICE), :],
            land0.at[col],
            cut_s.at[d],
            cut_r.at[col],
            (row, k),
        )

    def cut_from(d):
        k = mate(d)
        return remote(bucket.at[0, 0:SLICE, :], land0.at[k], cut_s.at[d], cut_r.at[k], (row, k))

    @pl.loop(1, COLS)
    def _(d):
        cut(d).start()

    land0[col] = bucket[0, pl.ds(pl.multiple_of(col * SLICE, SLICE), SLICE), :]

    @pl.loop(1, COLS)
    def _(k):
        pack(k)

    @pl.loop(1, COLS)
    def _(d):
        cut_from(d).wait_recv()

    @pl.when(col == 0)
    def _():
        front_own.wait()

    @pl.when(col != 0)
    def _():
        front_cut(1).wait_recv()

    at_row = col * SLICE + lax.broadcasted_iota(jnp.int32, (SLICE, B), 0)
    at_col = lax.broadcasted_iota(jnp.int32, (SLICE, B), 1)

    @pl.loop(0, COLS)
    def _(k):
        code = tab[k, 0]
        extent = code & 1023
        tile = (code >> 12) & 7
        inside = (at_row < extent) & (at_col < extent)
        part = jnp.where(inside, land0[k].astype(F32), 0.0)
        for a in range(4):
            fslice[a] = fslice[a] + jnp.where(tile == 2 * a, part, 0.0)

    def pivot_row(d):
        here = pivot.at[zy, core]
        return remote(here, here, pr_s.at[d], pr_r, (fellow(d), col))

    @pl.when(row == 0)
    def _():
        pivot[zy, core] = fslice[0]

        @pl.loop(1, ROWS)
        def _(d):
            pivot_row(d).start()

    @pl.when(row != 0)
    def _():
        pivot_row(1).wait_recv()

    def pivot_col(d, there):
        here = pivot.at[there, core]
        return remote(here, here, pg_s.at[d], pg_r.at[there], (row, kin(d) * 2 + core))

    @pl.loop(1, ROWS)
    def _(d):
        pivot_col(d, zy).start()

    for a in range(4):
        col0[a, zy, core] = fslice[a]

    def gather(d, there):
        here = col0.at[:, there, core]
        return remote(here, here, ag_s.at[d], ag_r.at[there], (row, kin(d) * 2 + core))

    @pl.loop(1, ROWS)
    def _(d):
        gather(d, zy).start()

    @pl.loop(1, ROWS)
    def _(d):
        pivot_col(d, kin(d)).wait_recv()

    def pivot_swap(which):
        here = pivot.at[:, which]
        return remote(here, here, px.at[0], px.at[1], sibling)

    pivot_swap(core).start()

    def bulk(d):
        k = mate(d)
        return remote(bucket.at[k], land.at[col], bk_s.at[d], bk_r.at[col], (row, k))

    def bulk_from(d):
        k = mate(d)
        return remote(bucket.at[k], land.at[k], bk_s.at[d], bk_r.at[k], (row, k))

    @pl.loop(1, COLS)
    def _(d):
        bulk(d).start()

    keep_own = pltpu.make_async_copy(bucket.at[col], land.at[col], loc.at[2])
    keep_own.start()

    pivot_swap(1 - core).wait_recv()
    for i in range(4):
        for j in range(4):
            f = pivot[2 * i : 2 * i + 2, :, :, NB * j : NB * j + NB].reshape(NB, NB)
            g = pivot[2 * j : 2 * j + 2, :, :, NB * i : NB * i + NB].reshape(NB, NB)
            s[NB * i : NB * i + NB, NB * j : NB * j + NB] = 0.5 * (f + jnp.transpose(g))
    l_ref[...] = jnp.zeros_like(l_ref)
    v_ref[...] = jnp.zeros_like(v_ref)

    def gather_swap(which):
        here = col0.at[:, :, which]
        return remote(here, here, ax.at[0], ax.at[1], sibling)

    for j in range(4):
        factor_step(j, s, l_ref, v_ref)
        if j == 2:

            @pl.loop(1, ROWS)
            def _(d):
                gather(d, kin(d)).wait_recv()

            gather_swap(core).start()

    gather_swap(1 - core).wait_recv()

    @pl.loop(0, 16)
    def _(i):
        a = i // 4
        q = i % 4
        part = col0[a, pl.ds(q * 2, 2)].reshape(NB, B)
        out = pl.ds(pl.multiple_of(q * NB, NB), NB)
        panel[a, out, :] = dot_nt(part, v_ref[...])

    @pl.when(row == 0)
    def _():
        panel[0] = l_ref[...]

    panel_out = pltpu.make_async_copy(panel, panel_hbm, loc.at[3])
    panel_out.start()

    def need(d):
        return remote(own_need, need_hbm, nd_s.at[d], nd_r, (fellow(d), col))

    need_own = pltpu.make_async_copy(own_need, need_hbm, loc.at[4])

    @pl.when(row == col % ROWS)
    def _():
        for b in range(2):

            @pl.loop(0, 4)
            def _(q):
                part = pl.ds(pl.multiple_of(q * NB, NB), NB)
                own_need[b, part, :] = panel[col // ROWS + 2 * b, part, :].astype(BF16)

        need_own.start()

        @pl.loop(1, ROWS)
        def _(d):
            need(d).start()

        need_own.wait()

        @pl.loop(1, ROWS)
        def _(d):
            need(d).wait_send()

    @pl.when(row != col % ROWS)
    def _():
        need(1).wait_recv()

    @pl.when(row == 0)
    def _():
        @pl.loop(1, ROWS)
        def _(d):
            pivot_row(d).wait_send()

    @pl.when(col == 0)
    def _():
        @pl.loop(1, COLS)
        def _(d):
            front_cut(d).wait_send()

    pivot_swap(core).wait_send()
    gather_swap(core).wait_send()

    @pl.loop(1, ROWS)
    def _(d):
        pivot_col(d, zy).wait_send()
        gather(d, zy).wait_send()

    @pl.loop(1, COLS)
    def _(d):
        cut(d).wait_send()
        bulk(d).wait_send()

    @pl.loop(1, COLS)
    def _(d):
        bulk_from(d).wait_recv()

    keep_own.wait()
    panel_out.wait()


def main_call(tab, kids, front):
    any_space = pl.BlockSpec(memory_space=pl.ANY)
    dma = pltpu.SemaphoreType.DMA
    return pl.pallas_call(
        main_kernel,
        out_shape=(
            jax.ShapeDtypeStruct((COLS, B, B), BF16),
            jax.ShapeDtypeStruct((4, B, B), F32),
            jax.ShapeDtypeStruct((2, B, B), BF16),
        ),
        in_specs=[pl.BlockSpec(memory_space=pltpu.SMEM), any_space, any_space],
        out_specs=(any_space,) * 3,
        scratch_shapes=[
            pltpu.VMEM((8, B, B), BF16),
            pltpu.VMEM((COLS, B, B), BF16),
            pltpu.VMEM((COLS, SLICE, B), BF16),
            pltpu.VMEM((4, SLICE, B), F32),
            pltpu.VMEM((8, 2, SLICE, B), F32),
            pltpu.VMEM((4, 8, 2, SLICE, B), F32),
            pltpu.VMEM((B, B), F32),
            pltpu.VMEM((B, B), F32),
            pltpu.VMEM((B, B), F32),
            pltpu.VMEM((4, B, B), F32),
            pltpu.VMEM((2, B, B), BF16),
            dma((5,)),
            dma((COLS,)),
            dma((COLS,)),
            dma((COLS,)),
            dma,
            dma((ROWS,)),
            dma,
            dma((ROWS,)),
            dma((ROWS,)),
            dma((2,)),
            dma((ROWS,)),
            dma((ROWS,)),
            dma((2,)),
            dma((COLS,)),
            dma((COLS,)),
            dma((ROWS,)),
            dma,
        ],
        compiler_params=pltpu.CompilerParams(
            collective_id=0, has_side_effects=True, vmem_limit_bytes=56 * 2**20
        ),
        cost_estimate=pl.CostEstimate(
            flops=2 * 5 * B**3, bytes_accessed=24 * 2**20, transcendentals=0
        ),
    )(tab, kids, front)


def final_kernel(tab, front, panel, need, land, schur, panel_out, kids, sem):
    row = lax.axis_index("row")
    col = lax.axis_index("col")
    t = pl.program_id(0)
    a = t // 2
    b = t % 2

    def fetch(k):
        return pltpu.make_async_copy(land.at[k], kids.at[k], sem.at[k])

    @pl.when(t == 0)
    def _():
        @pl.loop(0, COLS)
        def _(k):
            @pl.when(tab[k, col] != 0)
            def _():
                fetch(k).start()

    @pl.when(b == 0)
    def _():
        panel_out[...] = panel[...]

    i = a * ROWS + row
    j = b * COLS + col
    keep = (i > 0) & (j > 0)

    @pl.loop(0, 4)
    def _(q):
        part = pl.ds(pl.multiple_of(q * NB, NB), NB)
        p = panel[0, part, :]
        hi = p.astype(BF16)
        lo = (p - hi.astype(F32)).astype(BF16)
        update = dot_nt(hi, need[0], None) + dot_nt(lo, need[0], None)
        schur[0, part, :] = jnp.where(keep, front[0, part, :] - update, 0.0)

    at_row = lax.broadcasted_iota(jnp.int32, (NB, B), 0)
    at_col = lax.broadcasted_iota(jnp.int32, (NB, B), 1)

    @pl.loop(0, COLS)
    def _(k):
        code = tab[k, col]
        extent = code & 1023

        @pl.when((code != 0) & (((code >> 12) & 7) == t))
        def _():
            fetch(k).wait()

            @pl.loop(0, 4)
            def _(q):
                part = pl.ds(pl.multiple_of(q * NB, NB), NB)
                inside = (at_row + q * NB < extent) & (at_col < extent) & keep
                schur[0, part, :] = schur[0, part, :] + jnp.where(
                    inside, kids[k, part, :].astype(F32), 0.0
                )


def final_call(tab, front, panel, need, land):
    return pl.pallas_call(
        final_kernel,
        out_shape=(
            jax.ShapeDtypeStruct((8, B, B), F32),
            jax.ShapeDtypeStruct((4, B, B), F32),
        ),
        grid_spec=pltpu.PrefetchScalarGridSpec(
            num_scalar_prefetch=1,
            grid=(8,),
            in_specs=[
                pl.BlockSpec((1, B, B), lambda t, tab: (t, 0, 0)),
                pl.BlockSpec((1, B, B), lambda t, tab: (t // 2, 0, 0)),
                pl.BlockSpec((1, B, B), lambda t, tab: (t % 2, 0, 0)),
                pl.BlockSpec(memory_space=pl.ANY),
            ],
            out_specs=[
                pl.BlockSpec((1, B, B), lambda t, tab: (t, 0, 0)),
                pl.BlockSpec((1, B, B), lambda t, tab: (t // 2, 0, 0)),
            ],
            scratch_shapes=[pltpu.VMEM((COLS, B, B), BF16), pltpu.SemaphoreType.DMA((COLS,))],
        ),
        compiler_params=pltpu.CompilerParams(vmem_limit_bytes=56 * 2**20),
        cost_estimate=pl.CostEstimate(
            flops=4 * 8 * B**3, bytes_accessed=36 * 2**20, transcendentals=0
        ),
    )(tab, front, panel, need, land)


def per_device(front_init, child_tiles, child_map, child_counts, child_extent):
    row = lax.axis_index("row")
    maps = lax.dynamic_index_in_dim(child_map, row, 0, False)
    counts = lax.dynamic_index_in_dim(child_counts, row, 0, False)
    extents = lax.dynamic_index_in_dim(child_extent, row, 0, False)
    slots = jnp.arange(8, dtype=jnp.int32)[None, :]
    tile = maps[:, :, 0] // ROWS * 2 + maps[:, :, 1] // COLS
    code = (1 << 20) + slots * (1 << 16) + tile * (1 << 12) + extents
    code = jnp.where(slots < counts[:, None], code, 0)
    dests = jnp.arange(COLS, dtype=jnp.int32)[None, None, :]
    hit = (maps[:, :, 1] % COLS)[:, :, None] == dests
    tab = jnp.sum(jnp.where(hit, code[:, :, None], 0), axis=1)
    kids = child_tiles.reshape(8, B, B)
    land, panel, need = main_call(tab, kids, front_init.reshape(4, 2, B, B))
    schur, panel = final_call(tab, front_init.reshape(8, B, B), panel, need, land)
    return schur.reshape(4, 1, 2, 1, B, B), panel.reshape(4, 1, B, B)


def solution(mesh):
    in_specs = (
        P(None, "row", None, "col", None, None),
        P("row", "col", None, None, None),
        P(),
        P(),
        P(),
    )
    out_specs = (P(None, "row", None, "col", None, None), P(None, "row", None, None))
    return jax.shard_map(
        per_device, mesh=mesh, in_specs=in_specs, out_specs=out_specs, check_vma=False
    )
```

time: 698 us -> 238 us (0.34)
  the two profiles are of different devices: /device:TPU:72 before, /device:TPU:107 now
where the time goes in v1:
time: 238 us
  Pallas kernels  234 us (98%)
    pallas_call x1, Pallas kernels, main_call(): pl.pallas_call(main_kernel, out_shape=(jax.ShapeDtypeStruct((COLS, B, B),...  211 us
    pallas_call x1, Pallas kernels, final_call(): pl.pallas_call(final_kernel, out_shape=(jax.ShapeDtypeStruct((8, B, B), F...  23.6 us

profile of v1, /device:TPU:107, one launch (start us, length us, event | category | flops | bytes accessed | tf_op | source)
XLA Modules:
  0.0 237.6 jit_solution(2584195665838435532)
XLA Ops:
  0.6 0.0 copy-start
  0.6 0.7 fusion.12
  1.4 0.1 copy-done
  1.5 0.8 fusion.8
  2.3 0.1 copy.13
  2.3 0.1 copy.14
  2.4 0.7 select_reduce_fusion.tab
  3.1 210.8 %shard_map.68 = (bf16[16,512,512]{2,1,0:T(8,128)(2,1)}, f32[4,512,512]{2,1,0:T(8,128)}, bf16[2,512,512]{2,1,0:T(8,128)(2,1)}) custom-call(s32[16,16]{1,0:T(8,128)} %select_reduce_fusion.tab, bf16[8,512,512]{2,1,0:T(8,128)(2,1)} %bitcast.22, f32[4,2,512,512]{3,2,1,0:T(8,128)} %bitcast.20), custom_call_target="tpu_custom_call" | custom-call | flops 1342177280 | bytes 25165824 | tf_op jit(solution)/shard_map/pallas_call | solution.py:407
  213.9 23.6 %shard_map.69 = (f32[8,512,512]{2,1,0:T(8,128)}, f32[4,512,512]{2,1,0:T(8,128)}) custom-call(s32[16,16]{1,0:T(8,128)} %select_reduce_fusion.tab, f32[8,512,512]{2,1,0:T(8,128)} %bitcast.21, f32[4,512,512]{2,1,0:T(8,128)} %get-tuple-element.7.panel, bf16[2,512,512]{2,1,0:T(8,128)(2,1)} %get-tuple-element.8.need, bf16[16,512,512]{2,1,0:T(8,128)(2,1)} %get-tuple-element.9.land), custom_call_target="tpu_custom_call" | custom-call | flops 4294967296 | bytes 37748736 | tf_op jit(solution)/shard_map/pallas_call | solution.py:512
  (4 shorter events, 0.0 us)
Async XLA Ops:
  0.6 0.8 copy-start

commit v2 on v1

v2 whole, which is shorter than its diff:
```python
import functools

import jax
import jax.numpy as jnp
from jax import lax
from jax.experimental import pallas as pl
from jax.experimental.pallas import tpu as pltpu
from jax.sharding import PartitionSpec as P

MESH = pl.DeviceIdType.MESH
HIGH = lax.Precision.HIGHEST
F32 = jnp.float32
BF16 = jnp.bfloat16
B = 512
NB = 128
SLICE = 32
COLS = 16
ROWS = 8
HOOKS = (0, 1)
BULK = ((), (), (), (1, 2, 3), (4, 5, 12, 13, 8, 9), (6, 7, 14, 15, 10, 11))


def dot_nt(a, b, precision=HIGH):
    return lax.dot_general(
        a, b, (((1,), (1,)), ((), ())), precision=precision, preferred_element_type=F32
    )


def dot_nn(a, b, precision=HIGH):
    return lax.dot_general(
        a, b, (((1,), (0,)), ((), ())), precision=precision, preferred_element_type=F32
    )


def wide(x):
    return jnp.broadcast_to(x, (8, NB))


def factor_block(s):
    lane = lax.broadcasted_iota(jnp.int32, (8, NB), 1)
    sub = lax.broadcasted_iota(jnp.int32, (8, NB), 0)
    groups = NB // 8
    rows = [s[8 * p : 8 * p + 8, :] for p in range(groups)]
    eye = [jnp.where(lane == sub + 8 * p, 1.0, 0.0).astype(F32) for p in range(groups)]
    out_u, out_v = [], []
    for p in range(groups):
        r, e = rows[p], eye[p]
        cols = [wide(r[:, 8 * p + t : 8 * p + t + 1]) for t in range(8)]
        inv = [jnp.where(sub == t, 1.0, 0.0).astype(F32) for t in range(8)]
        pivots = None
        for t in range(8):
            pivot = wide(cols[t][t : t + 1, :])
            pivots = pivot if t == 0 else jnp.where(sub == t, pivot, pivots)
            m = jnp.where(sub > t, cols[t], 0.0) * (1.0 / pivot)
            for j in range(t + 1, 8):
                cols[j] = cols[j] - m * wide(cols[j][t : t + 1, :])
            for j in range(t + 1):
                inv[j] = inv[j] - m * wide(inv[j][t : t + 1, :])
        scale = lax.rsqrt(pivots)
        u = jnp.zeros_like(r)
        v = jnp.zeros_like(e)
        for t in range(8):
            u = u + inv[t] * wide(r[t : t + 1, :])
            v = v + inv[t] * wide(e[t : t + 1, :])
        u = u * scale
        v = v * scale
        out_u.append(jnp.where(lane >= sub + 8 * p, u, 0.0))
        out_v.append(v)
        if p < groups - 1:
            ut = jnp.transpose(u)
            for q in range(p + 1, groups):
                coef = ut[8 * q : 8 * q + 8, :]
                for t in range(8):
                    c = wide(coef[:, t : t + 1])
                    rows[q] = rows[q] - c * wide(u[t : t + 1, :])
                    eye[q] = eye[q] - c * wide(v[t : t + 1, :])
    return jnp.concatenate(out_u, 0), jnp.concatenate(out_v, 0)


def factor_step(j, s, l_ref, v_ref):
    a, b = NB * j, NB * j + NB
    u, v = factor_block(s[a:b, a:b])
    l_ref[a:b, a:b] = jnp.transpose(u)
    v_ref[a:b, a:b] = v
    if j:
        w = dot_nn(l_ref[a:b, 0:a], v_ref[0:a, 0:a])
        v_ref[a:b, 0:a] = -dot_nn(v, w)
    if b < B:
        low = dot_nt(s[b:B, a:b], v)
        l_ref[b:B, a:b] = low
        s[b:B, b:B] = s[b:B, b:B] - dot_nt(low, low)


def main_kernel(
    tab,
    kids_hbm,
    front_hbm,
    land,
    panel_hbm,
    part_hbm,
    kids,
    bucket,
    land0,
    fslice,
    pivot,
    col0,
    s,
    l_ref,
    v_ref,
    panel,
    own_need,
    need,
    front,
    w_hi,
    w_lo,
    loc,
    f_in,
    f_out,
    cut_s,
    cut_r,
    fs_s,
    fs_r,
    ft_s,
    ft_r,
    pr_s,
    pr_r,
    pg_s,
    pg_r,
    px,
    ag_s,
    ag_r,
    ay,
    ax,
    bk_s,
    bk_r,
    nd_s,
    nd_t,
    nd_r,
):
    row = lax.axis_index("row")
    col = lax.axis_index("col")
    zy = col // 2
    core = col % 2
    z = zy // 2
    yh = zy % 2
    x = row % 4
    yl = row // 4

    def remote(src, dst, ss, rs, to):
        return pltpu.make_async_remote_copy(
            src_ref=src, dst_ref=dst, send_sem=ss, recv_sem=rs, device_id=to, device_id_type=MESH
        )

    def kin(d):
        z = lax.rem(zy // 2 + d // 2, 4)
        return z * 2 + lax.rem(zy + d, 2)

    def mate(d):
        return kin(d // 2) * 2 + lax.rem(core + d, 2)

    def fellow(d):
        x = lax.rem(row + d, 4)
        return lax.rem(row // 4 + d // 4, 2) * 4 + x

    sibling = (row, zy * 2 + 1 - core)

    load = pltpu.make_async_copy(kids_hbm, kids, loc.at[0])
    load.start()

    barrier = pltpu.get_barrier_semaphore()

    @pl.loop(1, COLS)
    def _(d):
        pl.semaphore_signal(barrier, inc=1, device_id=(row, mate(d)), device_id_type=MESH)

    @pl.loop(1, ROWS)
    def _(d):
        pl.semaphore_signal(barrier, inc=1, device_id=(fellow(d), col), device_id_type=MESH)

    pl.semaphore_wait(barrier, COLS - 1 + ROWS - 1)

    def first_part(k):
        return front_hbm.at[0, 0, pl.ds(pl.multiple_of(k * SLICE, SLICE), SLICE), :]

    def rest_part(k):
        return front_hbm.at[1:4, 0, pl.ds(pl.multiple_of(k * SLICE, SLICE), SLICE), :]

    def first_cut(d):
        k = mate(d)
        return remote(first_part(k), fslice.at[0], fs_s.at[d], fs_r, (row, k))

    def rest_cut(d):
        k = mate(d)
        return remote(rest_part(k), fslice.at[1:4], ft_s.at[d], ft_r, (row, k))

    first_own = pltpu.make_async_copy(first_part(col), fslice.at[0], loc.at[1])
    rest_own = pltpu.make_async_copy(rest_part(col), fslice.at[1:4], loc.at[4])

    @pl.when(col == 0)
    def _():
        first_own.start()

        @pl.loop(1, COLS)
        def _(d):
            first_cut(d).start()

    load.wait()

    def pack(k):
        slot = (tab[col, k] >> 16) & 7

        @pl.loop(0, 4)
        def _(q):
            part = pl.ds(pl.multiple_of(q * NB, NB), NB)
            bucket[k, part, :] = kids[slot, part, :]

    pack(0)

    def cut(d):
        k = mate(d)
        return remote(
            bucket.at[0, pl.ds(pl.multiple_of(k * SLICE, SLICE), SLICE), :],
            land0.at[col],
            cut_s.at[d],
            cut_r.at[col],
            (row, k),
        )

    def cut_from(d):
        k = mate(d)
        return remote(bucket.at[0, 0:SLICE, :], land0.at[k], cut_s.at[d], cut_r.at[k], (row, k))

    @pl.loop(1, COLS)
    def _(d):
        cut(d).start()

    def bulk(d):
        k = mate(d)
        return remote(bucket.at[k], land.at[col], bk_s.at[d], bk_r.at[col], (row, k))

    def bulk_from(d):
        k = mate(d)
        return remote(bucket.at[k], land.at[k], bk_s.at[d], bk_r.at[k], (row, k))

    keep_own = pltpu.make_async_copy(bucket.at[col], land.at[col], loc.at[2])

    def start_bulk(stage):
        for d in BULK[stage]:
            bulk(d).start()

    land0[col] = bucket[0, pl.ds(pl.multiple_of(col * SLICE, SLICE), SLICE), :]

    @pl.loop(1, COLS)
    def _(k):
        pack(k)

    keep_own.start()

    @pl.when(col == 0)
    def _():
        rest_own.start()

        @pl.loop(1, COLS)
        def _(d):
            rest_cut(d).start()

    def fetch(t):
        return pltpu.make_async_copy(front_hbm.at[t // 2, t % 2], front.at[t], f_in.at[t])

    for t in range(8):
        fetch(t).start()

    start_bulk(0)

    @pl.loop(1, COLS)
    def _(d):
        cut_from(d).wait_recv()

    @pl.when(col == 0)
    def _():
        first_own.wait()

    @pl.when(col != 0)
    def _():
        first_cut(1).wait_recv()

    at_row = col * SLICE + lax.broadcasted_iota(jnp.int32, (SLICE, B), 0)
    at_col = lax.broadcasted_iota(jnp.int32, (SLICE, B), 1)

    def add_kids(tiles):
        @pl.loop(0, COLS)
        def _(k):
            code = tab[k, 0]
            extent = code & 1023
            tile = (code >> 12) & 7
            inside = (at_row < extent) & (at_col < extent)
            part = jnp.where(inside, land0[k].astype(F32), 0.0)
            for a in tiles:
                fslice[a] = fslice[a] + jnp.where(tile == 2 * a, part, 0.0)

    add_kids((0,))

    def pivot_row(d):
        here = pivot.at[zy, core]
        return remote(here, here, pr_s.at[d], pr_r, (fellow(d), col))

    @pl.when(row == 0)
    def _():
        pivot[zy, core] = fslice[0]

        @pl.loop(1, ROWS)
        def _(d):
            pivot_row(d).start()

    @pl.when(row != 0)
    def _():
        pivot_row(1).wait_recv()

    def pivot_col(d, there):
        here = pivot.at[there, core]
        return remote(here, here, pg_s.at[d], pg_r.at[there], (row, kin(d) * 2 + core))

    @pl.loop(1, ROWS)
    def _(d):
        pivot_col(d, zy).start()

    start_bulk(1)

    @pl.when(col == 0)
    def _():
        rest_own.wait()

    @pl.when(col != 0)
    def _():
        rest_cut(1).wait_recv()

    add_kids((1, 2, 3))

    for a in range(4):
        col0[a, z, yh, core] = fslice[a]

    def gather(d, there):
        here = col0.at[:, there, yh, core]
        to = (row, lax.rem(z + d, 4) * 4 + yh * 2 + core)
        return remote(here, here, ag_s.at[d], ag_r.at[there], to)

    @pl.loop(1, 4)
    def _(d):
        gather(d, z).start()

    start_bulk(2)

    @pl.loop(1, ROWS)
    def _(d):
        pivot_col(d, kin(d)).wait_recv()

    def pivot_swap(which):
        here = pivot.at[:, which]
        return remote(here, here, px.at[0], px.at[1], sibling)

    pivot_swap(core).start()

    start_bulk(3)

    pivot_swap(1 - core).wait_recv()
    for i in range(4):
        for j in range(4):
            f = pivot[2 * i : 2 * i + 2, :, :, NB * j : NB * j + NB].reshape(NB, NB)
            g = pivot[2 * j : 2 * j + 2, :, :, NB * i : NB * i + NB].reshape(NB, NB)
            s[NB * i : NB * i + NB, NB * j : NB * j + NB] = 0.5 * (f + jnp.transpose(g))
    l_ref[...] = jnp.zeros_like(l_ref)
    v_ref[...] = jnp.zeros_like(v_ref)

    def cross(side):
        here = col0.at[:, :, side, core]
        return remote(here, here, ay.at[0], ay.at[1], (row, z * 4 + (1 - yh) * 2 + core))

    def gather_swap(side, which, n):
        here = col0.at[:, :, side, which]
        return remote(here, here, ax.at[2 * n], ax.at[2 * n + 1], sibling)

    def relay_cross():
        @pl.loop(1, 4)
        def _(d):
            gather(d, lax.rem(z + d, 4)).wait_recv()

        cross(yh).start()
        gather_swap(yh, core, 0).start()
        start_bulk(4)

    def relay_swap():
        cross(1 - yh).wait_recv()
        gather_swap(1 - yh, core, 1).start()
        start_bulk(5)

    hooks = {HOOKS[0]: relay_cross, HOOKS[1]: relay_swap}
    for j in range(4):
        factor_step(j, s, l_ref, v_ref)
        if j in hooks:
            hooks[j]()

    gather_swap(yh, 1 - core, 0).wait_recv()
    gather_swap(1 - yh, 1 - core, 1).wait_recv()

    for i in range(4):
        for j in range(i, 4):
            here = (slice(NB * i, NB * i + NB), slice(NB * j, NB * j + NB))
            w = jnp.transpose(v_ref[here[1], here[0]])
            hi = w.astype(BF16)
            w_hi[here] = hi
            w_lo[here] = (w - hi.astype(F32)).astype(BF16)
    for w in (w_hi, w_lo):
        w[NB : 2 * NB, 0:NB] = jnp.zeros((NB, NB), BF16)
        w[3 * NB : B, 2 * NB : 3 * NB] = jnp.zeros((NB, NB), BF16)

    half = B // 2

    @pl.loop(0, 4)
    def _(a):
        part = col0[a].reshape(B, B)
        hi = part.astype(BF16)
        lo = (part - hi.astype(F32)).astype(BF16)
        for c0, depth in ((0, half), (half, B)):
            wh = w_hi[0:depth, c0 : c0 + half]
            wl = w_lo[0:depth, c0 : c0 + half]
            panel[a, :, c0 : c0 + half] = (
                dot_nn(hi[:, 0:depth], wh, None)
                + dot_nn(hi[:, 0:depth], wl, None)
                + dot_nn(lo[:, 0:depth], wh, None)
            )

    @pl.when(row == 0)
    def _():
        panel[0] = l_ref[...]

    panel_out = pltpu.make_async_copy(panel, panel_hbm, loc.at[3])
    panel_out.start()

    root = col % ROWS

    def piece(ref, g):
        return ref.at[:, pl.ds(pl.multiple_of(g * NB, NB), NB), :]

    def beside(d):
        return lax.rem(x + d, 4)

    def deal(d):
        g = beside(d)
        to = (yl * 4 + g, col)
        return remote(piece(own_need, g), piece(need, g), nd_t.at[d], nd_r.at[g], to)

    def hand(d, ref, g):
        to = (yl * 4 + beside(d), col)
        return remote(piece(ref, g), piece(need, g), nd_s.at[d], nd_r.at[g], to)

    def over(ref):
        to = ((1 - yl) * 4 + x, col)
        return remote(piece(ref, x), piece(need, x), nd_s.at[0], nd_r.at[x], to)

    need_own = pltpu.make_async_copy(own_need, need, loc.at[5])

    @pl.when(row == root)
    def _():
        for b in range(2):
            for q in range(4):
                part = panel[col // ROWS + 2 * b, NB * q : NB * q + NB, :]
                own_need[b, :, NB * q : NB * q + NB] = jnp.transpose(part).astype(BF16)

        over(own_need).start()

        @pl.loop(1, 4)
        def _(d):
            deal(d).start()

        @pl.loop(1, 4)
        def _(d):
            hand(d, own_need, x).start()

        need_own.start()
        need_own.wait()
        over(own_need).wait_send()

        @pl.loop(1, 4)
        def _(d):
            deal(d).wait_send()
            hand(d, own_need, x).wait_send()

    @pl.when((row != root) & (yl == root // 4))
    def _():
        hand(1, need, x).wait_recv()
        over(need).start()

        @pl.loop(1, 4)
        def _(d):
            @pl.when(beside(d) != root % 4)
            def _():
                hand(d, need, x).start()

        @pl.loop(1, 4)
        def _(d):
            hand(d, need, beside(d)).wait_recv()

        over(need).wait_send()

        @pl.loop(1, 4)
        def _(d):
            @pl.when(beside(d) != root % 4)
            def _():
                hand(d, need, x).wait_send()

    @pl.when(yl != root // 4)
    def _():
        hand(1, need, x).wait_recv()

        @pl.loop(1, 4)
        def _(d):
            hand(d, need, x).start()

        @pl.loop(1, 4)
        def _(d):
            hand(d, need, beside(d)).wait_recv()

        @pl.loop(1, 4)
        def _(d):
            hand(d, need, x).wait_send()

    for t in range(8):
        fetch(t).wait()

    def put(t):
        return pltpu.make_async_copy(front.at[t], part_hbm.at[t], f_out.at[t])

    @pl.loop(0, 8)
    def _(t):
        a = t // 2
        b = t % 2
        keep = (a * ROWS + row > 0) & (b * COLS + col > 0)
        p = panel[a]
        hi = p.astype(BF16)
        lo = (p - hi.astype(F32)).astype(BF16)
        update = dot_nn(hi, need[b], None) + dot_nn(lo, need[b], None)
        front[t] = jnp.where(keep, front[t] - update, 0.0)
        put(t).start()

    @pl.when(row == 0)
    def _():
        @pl.loop(1, ROWS)
        def _(d):
            pivot_row(d).wait_send()

    @pl.when(col == 0)
    def _():
        @pl.loop(1, COLS)
        def _(d):
            first_cut(d).wait_send()
            rest_cut(d).wait_send()

    pivot_swap(core).wait_send()
    cross(yh).wait_send()
    gather_swap(yh, core, 0).wait_send()
    gather_swap(1 - yh, core, 1).wait_send()

    @pl.loop(1, ROWS)
    def _(d):
        pivot_col(d, zy).wait_send()

    @pl.loop(1, 4)
    def _(d):
        gather(d, z).wait_send()

    @pl.loop(1, COLS)
    def _(d):
        cut(d).wait_send()
        bulk(d).wait_send()

    @pl.loop(1, COLS)
    def _(d):
        bulk_from(d).wait_recv()

    keep_own.wait()
    panel_out.wait()
    for t in range(8):
        put(t).wait()


def main_call(tab, kids, front):
    any_space = pl.BlockSpec(memory_space=pl.ANY)
    dma = pltpu.SemaphoreType.DMA
    return pl.pallas_call(
        main_kernel,
        out_shape=(
            jax.ShapeDtypeStruct((COLS, B, B), BF16),
            jax.ShapeDtypeStruct((4, B, B), F32),
            jax.ShapeDtypeStruct((8, B, B), F32),
        ),
        in_specs=[pl.BlockSpec(memory_space=pltpu.SMEM), any_space, any_space],
        out_specs=(any_space,) * 3,
        scratch_shapes=[
            pltpu.VMEM((8, B, B), BF16),
            pltpu.VMEM((COLS, B, B), BF16),
            pltpu.VMEM((COLS, SLICE, B), BF16),
            pltpu.VMEM((4, SLICE, B), F32),
            pltpu.VMEM((8, 2, SLICE, B), F32),
            pltpu.VMEM((4, 4, 2, 2, SLICE, B), F32),
            pltpu.VMEM((B, B), F32),
            pltpu.VMEM((B, B), F32),
            pltpu.VMEM((B, B), F32),
            pltpu.VMEM((4, B, B), F32),
            pltpu.VMEM((2, B, B), BF16),
            pltpu.VMEM((2, B, B), BF16),
            pltpu.VMEM((8, B, B), F32),
            pltpu.VMEM((B, B), BF16),
            pltpu.VMEM((B, B), BF16),
            dma((6,)),
            dma((8,)),
            dma((8,)),
            dma((COLS,)),
            dma((COLS,)),
            dma((COLS,)),
            dma,
            dma((COLS,)),
            dma,
            dma((ROWS,)),
            dma,
            dma((ROWS,)),
            dma((ROWS,)),
            dma((2,)),
            dma((4,)),
            dma((4,)),
            dma((2,)),
            dma((4,)),
            dma((COLS,)),
            dma((COLS,)),
            dma((4,)),
            dma((4,)),
            dma((4,)),
        ],
        compiler_params=pltpu.CompilerParams(
            collective_id=0, has_side_effects=True, vmem_limit_bytes=56 * 2**20
        ),
        cost_estimate=pl.CostEstimate(
            flops=2 * 5 * B**3, bytes_accessed=24 * 2**20, transcendentals=0
        ),
    )(tab, kids, front)


def final_kernel(
    tab, part_hbm, panel_hbm, land, schur_hbm, panel_out, acc, panel, kids, f_in, p_in, k_in, f_out, p_out
):
    row = lax.axis_index("row")
    col = lax.axis_index("col")

    def fetch(k, q):
        part = pl.ds(pl.multiple_of(q * NB, NB), NB)
        return pltpu.make_async_copy(land.at[k, part], kids.at[k, part], k_in.at[k, q])

    def fetch_front(t):
        return pltpu.make_async_copy(part_hbm.at[t], acc.at[t], f_in.at[t])

    def fetch_panel(a):
        return pltpu.make_async_copy(panel_hbm.at[a], panel.at[a], p_in.at[a])

    def put_panel(a):
        return pltpu.make_async_copy(panel.at[a], panel_out.at[a], p_out.at[a])

    def put(t):
        return pltpu.make_async_copy(acc.at[t], schur_hbm.at[t], f_out.at[t])

    for a in range(4):
        fetch_panel(a).start()
        fetch_front(2 * a).start()
        fetch_front(2 * a + 1).start()

    @pl.loop(0, COLS)
    def _(k):
        extent = tab[k, col] & 1023

        @pl.loop(0, 4)
        def _(q):
            @pl.when(q * NB < extent)
            def _():
                fetch(k, q).start()

    at_row = lax.broadcasted_iota(jnp.int32, (NB, B), 0)
    at_col = lax.broadcasted_iota(jnp.int32, (NB, B), 1)

    @pl.loop(0, 8)
    def _(t):
        a = t // 2
        b = t % 2

        @pl.when(b == 0)
        def _():
            fetch_panel(a).wait()
            put_panel(a).start()

        fetch_front(t).wait()
        i = a * ROWS + row
        j = b * COLS + col
        keep = (i > 0) & (j > 0)

        @pl.loop(0, COLS)
        def _(k):
            code = tab[k, col]
            extent = code & 1023

            @pl.when((code != 0) & (((code >> 12) & 7) == t))
            def _():
                @pl.loop(0, 4)
                def _(q):
                    @pl.when(q * NB < extent)
                    def _():
                        fetch(k, q).wait()
                        part = pl.ds(pl.multiple_of(q * NB, NB), NB)
                        inside = (at_row + q * NB < extent) & (at_col < extent) & keep
                        acc[t, part, :] = acc[t, part, :] + jnp.where(
                            inside, kids[k, part, :].astype(F32), 0.0
                        )

        put(t).start()

    for a in range(4):
        put_panel(a).wait()
    for t in range(8):
        put(t).wait()


def final_call(tab, partial, panel, land):
    any_space = pl.BlockSpec(memory_space=pl.ANY)
    dma = pltpu.SemaphoreType.DMA
    return pl.pallas_call(
        final_kernel,
        out_shape=(
            jax.ShapeDtypeStruct((8, B, B), F32),
            jax.ShapeDtypeStruct((4, B, B), F32),
        ),
        in_specs=[pl.BlockSpec(memory_space=pltpu.SMEM)] + [any_space] * 3,
        out_specs=(any_space, any_space),
        scratch_shapes=[
            pltpu.VMEM((8, B, B), F32),
            pltpu.VMEM((4, B, B), F32),
            pltpu.VMEM((COLS, B, B), BF16),
            dma((8,)),
            dma((4,)),
            dma((COLS, 4)),
            dma((8,)),
            dma((4,)),
        ],
        compiler_params=pltpu.CompilerParams(vmem_limit_bytes=56 * 2**20),
        cost_estimate=pl.CostEstimate(
            flops=8 * B**2, bytes_accessed=36 * 2**20, transcendentals=0
        ),
    )(tab, partial, panel, land)


def per_device(front_init, child_tiles, child_map, child_counts, child_extent):
    row = lax.axis_index("row")
    maps = lax.dynamic_index_in_dim(child_map, row, 0, False)
    counts = lax.dynamic_index_in_dim(child_counts, row, 0, False)
    extents = lax.dynamic_index_in_dim(child_extent, row, 0, False)
    slots = jnp.arange(8, dtype=jnp.int32)[None, :]
    tile = maps[:, :, 0] // ROWS * 2 + maps[:, :, 1] // COLS
    code = (1 << 20) + slots * (1 << 16) + tile * (1 << 12) + extents
    code = jnp.where(slots < counts[:, None], code, 0)
    dests = jnp.arange(COLS, dtype=jnp.int32)[None, None, :]
    hit = (maps[:, :, 1] % COLS)[:, :, None] == dests
    tab = jnp.sum(jnp.where(hit, code[:, :, None], 0), axis=1)
    kids = child_tiles.reshape(8, B, B)
    land, panel, partial = main_call(tab, kids, front_init.reshape(4, 2, B, B))
    schur, panel = final_call(tab, partial, panel, land)
    return schur.reshape(4, 1, 2, 1, B, B), panel.reshape(4, 1, B, B)


def solution(mesh):
    in_specs = (
        P(None, "row", None, "col", None, None),
        P("row", "col", None, None, None),
        P(),
        P(),
        P(),
    )
    out_specs = (P(None, "row", None, "col", None, None), P(None, "row", None, None))
    return jax.shard_map(
        per_device, mesh=mesh, in_specs=in_specs, out_specs=out_specs, check_vma=False
    )
```

time: 238 us -> 203 us (0.85)
  the two profiles are of different devices: /device:TPU:107 before, /device:TPU:72 now
where the time goes in v2:
time: 203 us; the launch traced here: 202 us
  Pallas kernels  199 us (98%)
    pallas_call x1, Pallas kernels, main_call(): pl.pallas_call(main_kernel, out_shape=(jax.ShapeDtypeStruct((COLS, B, B),...  184 us
    pallas_call x1, Pallas kernels, final_call(): pl.pallas_call(final_kernel, out_shape=(jax.ShapeDtypeStruct((8, B, B), F...  15 us

profile of v2, /device:TPU:72, one launch (start us, length us, event | category | flops | bytes accessed | tf_op | source)
XLA Modules:
  0.0 202.3 jit_solution(2667673254714564781)
XLA Ops:
  0.6 0.0 copy-start
  0.6 0.7 fusion.12
  1.4 0.1 copy-done
  1.5 0.8 fusion.8
  2.3 0.1 copy.13
  2.3 0.1 copy.14
  2.4 0.7 select_reduce_fusion.tab
  3.1 184.0 %shard_map.68 = (bf16[16,512,512]{2,1,0:T(8,128)(2,1)}, f32[4,512,512]{2,1,0:T(8,128)}, f32[8,512,512]{2,1,0:T(8,128)}) custom-call(s32[16,16]{1,0:T(8,128)} %select_reduce_fusion.tab, bf16[8,512,512]{2,1,0:T(8,128)(2,1)} %bitcast.20, f32[4,2,512,512]{3,2,1,0:T(8,128)} %bitcast.19), custom_call_target="tpu_custom_call" | custom-call | flops 1342177280 | bytes 25165824 | tf_op jit(solution)/shard_map/pallas_call | solution.py:589
  187.1 15.0 %shard_map.69 = (f32[8,512,512]{2,1,0:T(8,128)}, f32[4,512,512]{2,1,0:T(8,128)}) custom-call(s32[16,16]{1,0:T(8,128)} %select_reduce_fusion.tab, f32[8,512,512]{2,1,0:T(8,128)} %get-tuple-element.7.part_hbm, f32[4,512,512]{2,1,0:T(8,128)} %get-tuple-element.8.panel_hbm, bf16[16,512,512]{2,1,0:T(8,128)(2,1)} %get-tuple-element.9.land), custom_call_target="tpu_custom_call" | custom-call | flops 2097152 | bytes 37748736 | tf_op jit(solution)/shard_map/pallas_call | solution.py:731
  (4 shorter events, 0.0 us)
Async XLA Ops:
  0.6 0.8 copy-start

commit v3 on v2

--- a/solution.py
+++ b/solution.py
@@ -17,7 +17,7 @@
 COLS = 16
 ROWS = 8
 HOOKS = (0, 1)
-BULK = ((), (), (), (1, 2, 3), (4, 5, 12, 13, 8, 9), (6, 7, 14, 15, 10, 11))
+BULK = ((), (), (), (1, 2, 3, 6, 7), (14, 15, 10, 11, 4, 5, 12, 13, 8, 9), (), ())
 
 
 def dot_nt(a, b, precision=HIGH):
@@ -127,9 +127,11 @@
     pg_s,
     pg_r,
     px,
-    ag_s,
-    ag_r,
-    ay,
+    lz_s,
+    lz_r,
+    hz_s,
+    hz_r,
+    gy,
     ax,
     bk_s,
     bk_r,
@@ -339,14 +341,32 @@
     for a in range(4):
         col0[a, z, yh, core] = fslice[a]
 
-    def gather(d, there):
-        here = col0.at[:, there, yh, core]
-        to = (row, lax.rem(z + d, 4) * 4 + yh * 2 + core)
-        return remote(here, here, ag_s.at[d], ag_r.at[there], to)
+    partner = (row, z * 4 + (1 - yh) * 2 + core)
+
+    def along(d):
+        return (row, lax.rem(z + d, 4) * 4 + yh * 2 + core)
+
+    def low_z(d, there):
+        here = col0.at[0:2, there, yh, core]
+        return remote(here, here, lz_s.at[d], lz_r.at[there], along(d))
+
+    def low_y(side):
+        here = col0.at[0:2, :, side, core]
+        return remote(here, here, gy.at[0], gy.at[1], partner)
+
+    def high_y(side):
+        here = col0.at[2:4, z, side, core]
+        return remote(here, here, gy.at[2], gy.at[3], partner)
+
+    def high_z(d, there):
+        here = col0.at[2:4, there, :, core]
+        return remote(here, here, hz_s.at[d], hz_r.at[there], along(d))
+
+    high_y(yh).start()
 
     @pl.loop(1, 4)
     def _(d):
-        gather(d, z).start()
+        low_z(d, z).start()
 
     start_bulk(2)
 
@@ -371,26 +391,32 @@
     l_ref[...] = jnp.zeros_like(l_ref)
     v_ref[...] = jnp.zeros_like(v_ref)
 
-    def cross(side):
-        here = col0.at[:, :, side, core]
-        return remote(here, here, ay.at[0], ay.at[1], (row, z * 4 + (1 - yh) * 2 + core))
-
-    def gather_swap(side, which, n):
-        here = col0.at[:, :, side, which]
-        return remote(here, here, ax.at[2 * n], ax.at[2 * n + 1], sibling)
+    def gather_swap(which):
+        here = col0.at[:, :, :, which]
+        return remote(here, here, ax.at[0], ax.at[1], sibling)
 
     def relay_cross():
-        @pl.loop(1, 4)
-        def _(d):
-            gather(d, lax.rem(z + d, 4)).wait_recv()
-
-        cross(yh).start()
-        gather_swap(yh, core, 0).start()
+        high_y(1 - yh).wait_recv()
+
+        @pl.loop(1, 4)
+        def _(d):
+            high_z(d, z).start()
+
+        @pl.loop(1, 4)
+        def _(d):
+            low_z(d, lax.rem(z + d, 4)).wait_recv()
+
+        low_y(yh).start()
         start_bulk(4)
 
     def relay_swap():
-        cross(1 - yh).wait_recv()
-        gather_swap(1 - yh, core, 1).start()
+        low_y(1 - yh).wait_recv()
+
+        @pl.loop(1, 4)
+        def _(d):
+            high_z(d, lax.rem(z + d, 4)).wait_recv()
+
+        gather_swap(core).start()
         start_bulk(5)
 
     hooks = {HOOKS[0]: relay_cross, HOOKS[1]: relay_swap}
@@ -399,8 +425,7 @@
         if j in hooks:
             hooks[j]()
 
-    gather_swap(yh, 1 - core, 0).wait_recv()
-    gather_swap(1 - yh, 1 - core, 1).wait_recv()
+    gather_swap(1 - core).wait_recv()
 
     for i in range(4):
         for j in range(i, 4):
@@ -415,28 +440,20 @@
 
     half = B // 2
 
-    @pl.loop(0, 4)
-    def _(a):
-        part = col0[a].reshape(B, B)
+    root = col % ROWS
+
+    def solve(part, put):
         hi = part.astype(BF16)
         lo = (part - hi.astype(F32)).astype(BF16)
         for c0, depth in ((0, half), (half, B)):
             wh = w_hi[0:depth, c0 : c0 + half]
             wl = w_lo[0:depth, c0 : c0 + half]
-            panel[a, :, c0 : c0 + half] = (
+            put(
+                c0,
                 dot_nn(hi[:, 0:depth], wh, None)
                 + dot_nn(hi[:, 0:depth], wl, None)
-                + dot_nn(lo[:, 0:depth], wh, None)
+                + dot_nn(lo[:, 0:depth], wh, None),
             )
-
-    @pl.when(row == 0)
-    def _():
-        panel[0] = l_ref[...]
-
-    panel_out = pltpu.make_async_copy(panel, panel_hbm, loc.at[3])
-    panel_out.start()
-
-    root = col % ROWS
 
     def piece(ref, g):
         return ref.at[:, pl.ds(pl.multiple_of(g * NB, NB), NB), :]
@@ -461,10 +478,15 @@
 
     @pl.when(row == root)
     def _():
-        for b in range(2):
-            for q in range(4):
-                part = panel[col // ROWS + 2 * b, NB * q : NB * q + NB, :]
-                own_need[b, :, NB * q : NB * q + NB] = jnp.transpose(part).astype(BF16)
+        @pl.loop(0, 2)
+        def _(b):
+            def put_need(c0, value):
+                for q in range(4):
+                    own_need[b, c0 : c0 + half, NB * q : NB * q + NB] = jnp.transpose(
+                        value[NB * q : NB * q + NB, :]
+                    ).astype(BF16)
+
+            solve(col0[col // ROWS + 2 * b].reshape(B, B), put_need)
 
         over(own_need).start()
 
@@ -477,13 +499,6 @@
             hand(d, own_need, x).start()
 
         need_own.start()
-        need_own.wait()
-        over(own_need).wait_send()
-
-        @pl.loop(1, 4)
-        def _(d):
-            deal(d).wait_send()
-            hand(d, own_need, x).wait_send()
 
     @pl.when((row != root) & (yl == root // 4))
     def _():
@@ -496,6 +511,32 @@
             def _():
                 hand(d, need, x).start()
 
+    @pl.loop(0, 4)
+    def _(a):
+        def put_panel(c0, value):
+            panel[a, :, c0 : c0 + half] = value
+
+        solve(col0[a].reshape(B, B), put_panel)
+
+    @pl.when(row == 0)
+    def _():
+        panel[0] = l_ref[...]
+
+    panel_out = pltpu.make_async_copy(panel, panel_hbm, loc.at[3])
+    panel_out.start()
+
+    @pl.when(row == root)
+    def _():
+        need_own.wait()
+        over(own_need).wait_send()
+
+        @pl.loop(1, 4)
+        def _(d):
+            deal(d).wait_send()
+            hand(d, own_need, x).wait_send()
+
+    @pl.when((row != root) & (yl == root // 4))
+    def _():
         @pl.loop(1, 4)
         def _(d):
             hand(d, need, beside(d)).wait_recv()
@@ -523,6 +564,8 @@
         @pl.loop(1, 4)
         def _(d):
             hand(d, need, x).wait_send()
+
+    start_bulk(6)
 
     for t in range(8):
         fetch(t).wait()
@@ -556,9 +599,9 @@
             rest_cut(d).wait_send()
 
     pivot_swap(core).wait_send()
-    cross(yh).wait_send()
-    gather_swap(yh, core, 0).wait_send()
-    gather_swap(1 - yh, core, 1).wait_send()
+    low_y(yh).wait_send()
+    high_y(yh).wait_send()
+    gather_swap(core).wait_send()
 
     @pl.loop(1, ROWS)
     def _(d):
@@ -566,7 +609,8 @@
 
     @pl.loop(1, 4)
     def _(d):
-        gather(d, z).wait_send()
+        low_z(d, z).wait_send()
+        high_z(d, z).wait_send()
 
     @pl.loop(1, COLS)
     def _(d):
@@ -627,8 +671,10 @@
             dma((2,)),
             dma((4,)),
             dma((4,)),
+            dma((4,)),
+            dma((4,)),
+            dma((4,)),
             dma((2,)),
-            dma((4,)),
             dma((COLS,)),
             dma((COLS,)),
             dma((4,)),

time: 203 us -> 191 us (0.941)
  the two profiles are of different devices: /device:TPU:72 before, /device:TPU:38 now
where the time goes in v3:
time: 191 us
  Pallas kernels  188 us (98%)
    pallas_call x1, Pallas kernels, main_call(): pl.pallas_call(main_kernel, out_shape=(jax.ShapeDtypeStruct((COLS, B, B),...  173 us
    pallas_call x1, Pallas kernels, final_call(): pl.pallas_call(final_kernel, out_shape=(jax.ShapeDtypeStruct((8, B, B), F...  15.1 us

profile of v3, /device:TPU:38, one launch (start us, length us, event | category | flops | bytes accessed | tf_op | source)
XLA Modules:
  0.0 191.1 jit_solution(9237496475792457821)
XLA Ops:
  0.6 0.0 copy-start
  0.6 0.7 fusion.12
  1.4 0.1 copy-done
  1.5 0.8 fusion.8
  2.3 0.1 copy.13
  2.3 0.1 copy.14
  2.4 0.7 select_reduce_fusion.tab
  3.1 172.7 %shard_map.68 = (bf16[16,512,512]{2,1,0:T(8,128)(2,1)}, f32[4,512,512]{2,1,0:T(8,128)}, f32[8,512,512]{2,1,0:T(8,128)}) custom-call(s32[16,16]{1,0:T(8,128)} %select_reduce_fusion.tab, bf16[8,512,512]{2,1,0:T(8,128)(2,1)} %bitcast.20, f32[4,2,512,512]{3,2,1,0:T(8,128)} %bitcast.19), custom_call_target="tpu_custom_call" | custom-call | flops 1342177280 | bytes 25165824 | tf_op jit(solution)/shard_map/pallas_call | solution.py:633
  175.9 15.1 %shard_map.69 = (f32[8,512,512]{2,1,0:T(8,128)}, f32[4,512,512]{2,1,0:T(8,128)}) custom-call(s32[16,16]{1,0:T(8,128)} %select_reduce_fusion.tab, f32[8,512,512]{2,1,0:T(8,128)} %get-tuple-element.7.part_hbm, f32[4,512,512]{2,1,0:T(8,128)} %get-tuple-element.8.panel_hbm, bf16[16,512,512]{2,1,0:T(8,128)(2,1)} %get-tuple-element.9.land), custom_call_target="tpu_custom_call" | custom-call | flops 2097152 | bytes 37748736 | tf_op jit(solution)/shard_map/pallas_call | solution.py:777
  (4 shorter events, 0.0 us)
Async XLA Ops:
  0.6 0.8 copy-start

commit v4 on v3

--- a/solution.py
+++ b/solution.py
@@ -16,8 +16,8 @@
 SLICE = 32
 COLS = 16
 ROWS = 8
-HOOKS = (0, 1)
-BULK = ((), (), (), (1, 2, 3, 6, 7), (14, 15, 10, 11, 4, 5, 12, 13, 8, 9), (), ())
+HOOK = 1
+BULK = ((), (), (), (), (1, 2, 3, 4, 5), (12, 13, 8, 9), (6, 7, 14, 15, 10, 11))
 
 
 def dot_nt(a, b, precision=HIGH):
@@ -380,7 +380,35 @@
 
     pivot_swap(core).start()
 
-    start_bulk(3)
+    def gather_swap(which):
+        here = col0.at[:, :, :, which]
+        return remote(here, here, ax.at[0], ax.at[1], sibling)
+
+    def relay_cross():
+        high_y(1 - yh).wait_recv()
+
+        @pl.loop(1, 4)
+        def _(d):
+            high_z(d, z).start()
+
+        @pl.loop(1, 4)
+        def _(d):
+            low_z(d, lax.rem(z + d, 4)).wait_recv()
+
+        low_y(yh).start()
+        start_bulk(4)
+
+    def relay_swap():
+        low_y(1 - yh).wait_recv()
+
+        @pl.loop(1, 4)
+        def _(d):
+            high_z(d, lax.rem(z + d, 4)).wait_recv()
+
+        gather_swap(core).start()
+        start_bulk(5)
+
+    relay_cross()
 
     pivot_swap(1 - core).wait_recv()
     for i in range(4):
@@ -391,35 +419,7 @@
     l_ref[...] = jnp.zeros_like(l_ref)
     v_ref[...] = jnp.zeros_like(v_ref)
 
-    def gather_swap(which):
-        here = col0.at[:, :, :, which]
-        return remote(here, here, ax.at[0], ax.at[1], sibling)
-
-    def relay_cross():
-        high_y(1 - yh).wait_recv()
-
-        @pl.loop(1, 4)
-        def _(d):
-            high_z(d, z).start()
-
-        @pl.loop(1, 4)
-        def _(d):
-            low_z(d, lax.rem(z + d, 4)).wait_recv()
-
-        low_y(yh).start()
-        start_bulk(4)
-
-    def relay_swap():
-        low_y(1 - yh).wait_recv()
-
-        @pl.loop(1, 4)
-        def _(d):
-            high_z(d, lax.rem(z + d, 4)).wait_recv()
-
-        gather_swap(core).start()
-        start_bulk(5)
-
-    hooks = {HOOKS[0]: relay_cross, HOOKS[1]: relay_swap}
+    hooks = {HOOK: relay_swap}
     for j in range(4):
         factor_step(j, s, l_ref, v_ref)
         if j in hooks:
@@ -499,6 +499,7 @@
             hand(d, own_need, x).start()
 
         need_own.start()
+        start_bulk(6)
 
     @pl.when((row != root) & (yl == root // 4))
     def _():
@@ -510,6 +511,8 @@
             @pl.when(beside(d) != root % 4)
             def _():
                 hand(d, need, x).start()
+
+        start_bulk(6)
 
     @pl.loop(0, 4)
     def _(a):
@@ -557,6 +560,8 @@
         def _(d):
             hand(d, need, x).start()
 
+        start_bulk(6)
+
         @pl.loop(1, 4)
         def _(d):
             hand(d, need, beside(d)).wait_recv()
@@ -564,8 +569,6 @@
         @pl.loop(1, 4)
         def _(d):
             hand(d, need, x).wait_send()
-
-    start_bulk(6)
 
     for t in range(8):
         fetch(t).wait()

time: 191 us -> 188 us (0.984)
  the two profiles are of different devices: /device:TPU:38 before, /device:TPU:93 now
where the time goes in v4:
time: 188 us
  Pallas kernels  184 us (98%)
    pallas_call x1, Pallas kernels, main_call(): pl.pallas_call(main_kernel, out_shape=(jax.ShapeDtypeStruct((COLS, B, B),...  173 us
    pallas_call x1, Pallas kernels, final_call(): pl.pallas_call(final_kernel, out_shape=(jax.ShapeDtypeStruct((8, B, B), F...  11.5 us

profile of v4, /device:TPU:93, one launch (start us, length us, event | category | flops | bytes accessed | tf_op | source)
XLA Modules:
  0.0 187.5 jit_solution(11409448021078435135)
XLA Ops:
  0.6 0.0 copy-start
  0.6 0.7 fusion.12
  1.4 0.1 copy-done
  1.5 0.8 fusion.8
  2.3 0.1 copy.13
  2.3 0.1 copy.14
  2.4 0.7 select_reduce_fusion.tab
  3.1 172.7 %shard_map.68 = (bf16[16,512,512]{2,1,0:T(8,128)(2,1)}, f32[4,512,512]{2,1,0:T(8,128)}, f32[8,512,512]{2,1,0:T(8,128)}) custom-call(s32[16,16]{1,0:T(8,128)} %select_reduce_fusion.tab, bf16[8,512,512]{2,1,0:T(8,128)(2,1)} %bitcast.20, f32[4,2,512,512]{3,2,1,0:T(8,128)} %bitcast.19), custom_call_target="tpu_custom_call" | custom-call | flops 1342177280 | bytes 25165824 | tf_op jit(solution)/shard_map/pallas_call | solution.py:636
  175.9 11.5 %shard_map.69 = (f32[8,512,512]{2,1,0:T(8,128)}, f32[4,512,512]{2,1,0:T(8,128)}) custom-call(s32[16,16]{1,0:T(8,128)} %select_reduce_fusion.tab, f32[8,512,512]{2,1,0:T(8,128)} %get-tuple-element.7.part_hbm, f32[4,512,512]{2,1,0:T(8,128)} %get-tuple-element.8.panel_hbm, bf16[16,512,512]{2,1,0:T(8,128)(2,1)} %get-tuple-element.9.land), custom_call_target="tpu_custom_call" | custom-call | flops 2097152 | bytes 37748736 | tf_op jit(solution)/shard_map/pallas_call | solution.py:780
  (4 shorter events, 0.0 us)
Async XLA Ops:
  0.6 0.8 copy-start
